TPU v7x, 512 devices: a whole 4x8x8 slice. The times are simulated.
512 devices in a mesh: ctx: 64 (over z, x, core), head: 8 (over y).
Axes of the slice: x: 4, y: 8, z: 8, core: 2. Of those that a mesh axis runs over, the one named last changes fastest.
Arguments:
- hidden: bfloat16 [65536, 2048], P('ctx'), may hold values from -16 to 16
- qkv_weight: bfloat16 [2048, 3072], P('ctx', 'head'), may hold values from -0.125 to 0.125
- out_grad: float32 [65536, 1024], P('ctx', 'head'), may hold values from -6 to 6
Outputs:
- attended: float32 [65536, 1024], P('ctx', 'head')
- weight_grad: float32 [2048, 3072], P('ctx', 'head')
All inputs are finite; a program needn't handle non-finite values.
Results may differ from a plain program's by a relative error of at most 0.0018.
Values may be sent and summed in bfloat16 or wider, within the bound.
No kernel may reach another device: no remote copies, remote signals or barrier semaphores. Data moves between devices by JAX's collectives and lax.ppermute only.
A program may use at most 64 MiB of HBM per device.

v0:
```python
import jax
import jax.numpy as jnp
from jax import lax
from jax.sharding import PartitionSpec as P

HD = 128
BLOCK = 128
HIGH = lax.Precision.HIGHEST


def prefix_2(part, axis, combine, identity, reverse):
    count = lax.axis_size(axis)
    place = lax.axis_index(axis)
    ahead = count - 1 - place if reverse else place
    gathered = lax.all_gather(part, axis)
    state = jnp.zeros_like(part) + jnp.asarray(identity, part.dtype)

    def one(step, state):
        source = count - 1 - step if reverse else step
        return combine(state, lax.dynamic_index_in_dim(gathered, source, 0, False))

    return lax.fori_loop(0, ahead, one, state)


def local(hidden, qkv_weight, out_grad):
    tokens = hidden.shape[0]
    columns = qkv_weight.shape[1]
    heads = columns // (3 * HD)
    total_tokens = tokens * lax.axis_size("ctx")
    scale = float(HD * total_tokens) ** (-0.5)
    grad_scale = float(total_tokens) ** (-0.5)
    inputs = hidden
    proj = jnp.dot(
        inputs,
        lax.all_gather(qkv_weight, "ctx", axis=0, tiled=True),
        preferred_element_type=jnp.float32,
    )
    count = tokens // BLOCK
    proj = proj.reshape(count, BLOCK, heads, 3, HD)
    query = proj[:, :, :, 0]
    keys = proj[:, :, :, 1]
    values = proj[:, :, :, 2]
    cotangent = out_grad.reshape(count, BLOCK, heads, HD)
    kv_block = jnp.einsum("nshd,nshe->nhde", keys, values, precision=HIGH)
    qg_block = jnp.einsum("nthd,nthe->nhde", query, cotangent, precision=HIGH)
    kv_total = jnp.sum(kv_block, axis=0)
    qg_total = jnp.sum(qg_block, axis=0)
    zeros_state = jnp.zeros_like(kv_total)
    before = prefix_2(kv_total, "ctx", lambda a, b: a + b, zeros_state, False)
    after = prefix_2(qg_total, "ctx", lambda a, b: a + b, zeros_state, True)
    prefix = before[None] + jnp.cumsum(kv_block, axis=0) - kv_block
    suffix = after[None] + qg_total[None] - jnp.cumsum(qg_block, axis=0)
    rows = jnp.arange(BLOCK)
    mask = (rows[:, None] >= rows[None, :]).astype(jnp.float32)
    scores = jnp.einsum("nthd,nshd->nhts", query, keys, precision=HIGH) * mask
    inner = jnp.einsum("nhts,nshe->nthe", scores, values, precision=HIGH)
    carried = jnp.einsum("nthd,nhde->nthe", query, prefix, precision=HIGH)
    attended = (scale * (inner + carried)).reshape(tokens, heads * HD)
    dmat = jnp.einsum("nthe,nshe->nhts", cotangent, values, precision=HIGH) * mask
    dquery = scale * (
        jnp.einsum("nhts,nshd->nthd", dmat, keys, precision=HIGH)
        + jnp.einsum("nthe,nhde->nthd", cotangent, prefix, precision=HIGH)
    )
    dkeys = scale * (
        jnp.einsum("nhts,nthd->nshd", dmat, query, precision=HIGH)
        + jnp.einsum("nshe,nhde->nshd", values, suffix, precision=HIGH)
    )
    dvalues = scale * (
        jnp.einsum("nhts,nthe->nshe", scores, cotangent, precision=HIGH)
        + jnp.einsum("nshd,nhde->nshe", keys, suffix, precision=HIGH)
    )
    dproj = (
        jnp.stack([dquery, dkeys, dvalues], axis=3).reshape(tokens, columns).astype(jnp.bfloat16)
    )
    inputs = hidden
    product = lax.dot_general(
        inputs, dproj, (((0,), (0,)), ((), ())), preferred_element_type=jnp.float32
    )
    weight_grad = lax.psum_scatter(product * grad_scale, "ctx", scatter_dimension=0, tiled=True)
    return (attended, weight_grad)


def solution(mesh):
    return jax.shard_map(
        local,
        mesh=mesh,
        in_specs=(P("ctx", None), P("ctx", "head"), P("ctx", "head")),
        out_specs=(P("ctx", "head"), P("ctx", "head")),
        check_vma=False,
    )
```

profile of v0, /device:TPU:8, one launch (start us, length us, event | category | flops | bytes accessed | tf_op | source)
XLA Modules:
  0.0 499.1 jit_solution(4324925228339906326)
XLA Ops:
  8.0 91.0 %all-gather.6.cloned.1.call-done = bf16[2048,384]{1,0:T(8,128)(2,1)} async-done(((bf16[32,384]{1,0:T(8,128)(2,1)}), bf16[2048,384]{1,0:T(8,128)(2,1)}) %all-gather.6.cloned.1.call-update) | async-done | bytes 1572880 | tf_op jit(solution)/shard_map/all_gather | solution.py:35
  99.0 4.5 convolution_bitcast_fusion
  104.4 1.6 fusion.33
  106.4 2.5 fusion.34
  108.9 1.2 fusion.5
  110.2 1.8 fusion.22
  112.0 1.4 fusion.15
  113.4 1.2 convolution_multiply_fusion
  114.6 1.8 convolution_bitcast_fusion.1
  116.4 72.2 %all-gather.8.cloned.1.call-done = f32[8192,128]{1,0:T(8,128)} async-done(((f32[128,128]{1,0:T(8,128)}), f32[8192,128]{1,0:T(8,128)}) %all-gather.8.cloned.1.call-update) | async-done | bytes 4194320 | tf_op jit(solution)/shard_map/all_gather | solution.py:15
  188.6 85.3 %all-gather.10.cloned.1.call-done = f32[8192,128]{1,0:T(8,128)} async-done(((f32[128,128]{1,0:T(8,128)}), f32[8192,128]{1,0:T(8,128)}) %all-gather.10.cloned.1.call-update) | async-done | bytes 4194320 | tf_op jit(solution)/shard_map/all_gather | solution.py:15
  274.0 55.6 %while.23 = (s32[]{:T(128)}, f32[1,128,128]{2,1,0:T(8,128)S(1)}, s32[]{:T(128)}, f32[64,1,128,128]{3,2,1,0:T(8,128)}, s32[]{:T(128)}, /*index=5*/s32[]{:T(128)}, s32[]{:T(128)}, s32[]{:T(128)}) while((s32[]{:T(128)}, f32[1,128,128]{2,1,0:T(8,128)S(1)}, s32[]{:T(128)}, f32[64,1,128,128]{3,2,1,0:T(8,128)}, s32[]{:T(128)}, /*index=5*/s32[]{:T(128)}, ...), condition=%wide.region_6.7_spmd, body=%wide.region_5.6_spmd.sunk | while | flops 16390 | bytes 196751 | solution.py:22
  281.0 0.9 bitcast_add_fusion.6
  283.7 0.9 bitcast_add_fusion.6
  329.6 1.2 reduce-window_subtract_fusion
  330.8 1.7 fusion.9
  332.5 1.2 fusion.10
  333.7 1.2 fusion.11
  335.0 1.0 pad_maximum_fusion
  335.9 2.4 copy.58
  338.3 5.9 %multiply_bitcast_fusion = f32[2048,384]{0,1:T(8,128)} fusion(bf16[1024,2048]{1,0:T(8,128)(2,1)} %param.7, bf16[48,8,8,128]{3,2,1,0:T(8,128)(2,1)} %bitcast.117), kind=kOutput, calls=%fused_computation.2 | convolution fusion | flops 1611399168 | bytes 8126464 | tf_op jit(solution)/shard_map/dot_general | solution.py:76
  344.2 3.6 copy.73
  348.4 1.4 fusion.4
  349.8 142.7 %reduce-scatter.4.cloned.1.call-done = f32[32,384]{1,0:T(8,128)} async-done(((f32[2048,384]{1,0:T(8,128)}), f32[32,384]{1,0:T(8,128)}) %reduce-scatter.4.cloned.1.call-update) | async-done | bytes 49168
  (89 shorter events, 55.0 us)
Async XLA Ops:
  7.2 99.2 %copy-start = (f32[1024,128]{1,0:T(8,128)S(1)}, f32[1024,128]{1,0:T(8,128)}, u32[]{:S(2)}) copy-start(f32[1024,128]{1,0:T(8,128)} %param.9) | copy-start | bytes 1572868
  7.2 91.8 %all-gather.6.cloned.1.call-start = ((), (), s32[]{:S(2)}) async-start(), calls=%async_computation.1 | async-start | bytes 1597440 | tf_op jit(solution)/shard_map/all_gather | solution.py:35
  7.9 180.7 %all-gather.8.cloned.1.call-start = ((), (), s32[]{:S(2)}) async-start(), calls=%async_computation.2 | async-start | bytes 4259840 | tf_op jit(solution)/shard_map/all_gather | solution.py:15
  106.1 167.9 %all-gather.10.cloned.1.call-start = ((), (), s32[]{:S(2)}) async-start(), calls=%async_computation.3 | async-start | bytes 4259840 | tf_op jit(solution)/shard_map/all_gather | solution.py:15
  108.9 383.7 %reduce-scatter.4.cloned.1.call-start = ((), (), s32[]{:S(2)}) async-start(), calls=%async_computation.4 | async-start | bytes 3194880
  113.4 216.2 %copy-start.3 = (f32[128,128]{1,0:T(8,128)S(1)}, f32[128,128]{1,0:T(8,128)}, u32[]{:S(2)}) copy-start(f32[128,128]{1,0:T(8,128)} %get-tuple-element.122) | copy-start | bytes 196612
  329.6 2.9 copy-start.2
  329.6 4.1 copy-start.1
Sparse Core Ops, SparseCore 0:
  11.4 87.5 all-gather.5
  106.2 82.4 all-gather.7
  192.0 81.9 all-gather.9
  347.9 144.5 reduce-scatter.3
where the time goes:
time: 502 us; the launch traced here: 499 us
  waiting for transfers between devices  392 us (78%)
  other arithmetic  56.2 us (11%)
  matrix products  28.1 us (6%)
  between operations  13.9 us (3%)
  local copies, waits for them, and re-layouts  7.09 us (1%)
    all_gather x2, waiting for transfers between devices, prefix_2(): gathered = lax.all_gather(part, axis)  158 us
    unnamed x5, waiting for transfers between devices  143 us
    all_gather x1, waiting for transfers between devices, local(): lax.all_gather(qkv_weight, 'ctx', axis=0, tiled=True)  91 us
    add x63, other arithmetic, local(): after = prefix_2(qg_total, 'ctx', lambda a, b: a + b, zeros_state, True)  54 us
  transfers between devices with their start and end apart: 4, of which 4 were waited for; matrix products, arithmetic and copies ran while one was open for 2% of the time, Pallas kernels for 0%

commit v1 on v0

--- a/solution.py
+++ b/solution.py
@@ -6,6 +6,14 @@
 HD = 128
 BLOCK = 128
 HIGH = lax.Precision.HIGHEST
+
+
+def gather_by_exchange(array, axis, dim):
+    size = lax.axis_size(axis)
+    repeats = [size if d == dim else 1 for d in range(array.ndim)]
+    return lax.all_to_all(
+        jnp.tile(array, repeats), axis, split_axis=dim, concat_axis=dim, tiled=True
+    )
 
 
 def prefix_2(part, axis, combine, identity, reverse):
@@ -31,9 +39,7 @@
     grad_scale = float(total_tokens) ** (-0.5)
     inputs = hidden
     proj = jnp.dot(
-        inputs,
-        lax.all_gather(qkv_weight, "ctx", axis=0, tiled=True),
-        preferred_element_type=jnp.float32,
+        inputs, gather_by_exchange(qkv_weight, "ctx", 0), preferred_element_type=jnp.float32
     )
     count = tokens // BLOCK
     proj = proj.reshape(count, BLOCK, heads, 3, HD)

time: 502 us -> 464 us (0.924)
  waiting for transfers between devices: 392 us -> 299 us
  blocking collectives: 0 us -> 53.7 us
    all_gather x1 -> x0, waiting for transfers between devices: 91 us -> none  [local(): lax.all_gather(qkv_weight, 'ctx', axis=0, tiled=True)]
    all_to_all x0 -> x1, blocking collectives: none -> 53.7 us  [gather_by_exchange(): lax.all_to_all(jnp.tile(array, repeats), axis, split_axis=dim, concat_axi...]
    unnamed x5 -> x4, waiting for transfers between devices: 143 us -> 142 us
  transfers between devices with their start and end apart: 4 -> 3, of which waited for: 4 -> 3; matrix products, arithmetic and copies ran while one was open for 2% -> 3% of each run, Pallas kernels for 0% -> 0%
where the time goes in v1:
time: 464 us; the launch traced here: 461 us
  waiting for transfers between devices  299 us (64%)
  other arithmetic  56.2 us (12%)
  blocking collectives  53.7 us (12%)
  matrix products  27.1 us (6%)
  between operations  13.9 us (3%)
  local copies, waits for them, and re-layouts  9.72 us (2%)
    all_gather x2, waiting for transfers between devices, prefix_2(): gathered = lax.all_gather(part, axis)  157 us
    unnamed x4, waiting for transfers between devices  142 us
    add x63, other arithmetic, local(): after = prefix_2(qg_total, 'ctx', lambda a, b: a + b, zeros_state, True)  54 us
    all_to_all x1, blocking collectives, gather_by_exchange(): lax.all_to_all(jnp.tile(array, repeats), axis, split_axis=dim, concat_axi...  53.7 us
  transfers between devices with their start and end apart: 3, of which 3 were waited for; matrix products, arithmetic and copies ran while one was open for 3% of the time, Pallas kernels for 0%

profile of v1, /device:TPU:8, one launch (start us, length us, event | category | flops | bytes accessed | tf_op | source)
XLA Modules:
  0.0 461.3 jit_solution(3566302659330294318)
XLA Ops:
  7.2 0.9 tile.2
  8.1 53.7 %all_to_all.9 = bf16[64,32,384]{2,1,0:T(8,128)(2,1)S(1)} all-to-all(bf16[64,32,384]{2,1,0:T(8,128)(2,1)S(1)} %tile.2), channel_id=1, replica_groups=mesh['ctx'=64,'head'=8] {'ctx'}, dimensions={0} | all-to-all | bytes 3145728 | tf_op jit(solution)/shard_map/all_to_all | solution.py:14
  61.9 1.6 copy.36
  63.5 4.6 convolution_bitcast_fusion
  68.1 1.6 fusion.20
  69.8 2.5 fusion.21
  72.4 1.2 fusion.5
  73.6 1.8 fusion.17
  75.4 1.4 fusion.18
  76.8 1.2 convolution_multiply_fusion
  78.1 1.8 convolution_bitcast_fusion.1
  79.9 71.3 %all-gather.5.cloned.1.call-done = f32[8192,128]{1,0:T(8,128)} async-done(((f32[128,128]{1,0:T(8,128)}), f32[8192,128]{1,0:T(8,128)}) %all-gather.5.cloned.1.call-update) | async-done | bytes 4194320 | tf_op jit(solution)/shard_map/all_gather | solution.py:23
  151.2 85.3 %all-gather.7.cloned.1.call-done = f32[8192,128]{1,0:T(8,128)} async-done(((f32[128,128]{1,0:T(8,128)}), f32[8192,128]{1,0:T(8,128)}) %all-gather.7.cloned.1.call-update) | async-done | bytes 4194320 | tf_op jit(solution)/shard_map/all_gather | solution.py:23
  236.5 55.6 %while.23 = (s32[]{:T(128)}, f32[1,128,128]{2,1,0:T(8,128)S(1)}, s32[]{:T(128)}, f32[64,1,128,128]{3,2,1,0:T(8,128)}, s32[]{:T(128)}, /*index=5*/s32[]{:T(128)}, s32[]{:T(128)}, s32[]{:T(128)}) while((s32[]{:T(128)}, f32[1,128,128]{2,1,0:T(8,128)S(1)}, s32[]{:T(128)}, f32[64,1,128,128]{3,2,1,0:T(8,128)}, s32[]{:T(128)}, /*index=5*/s32[]{:T(128)}, ...), condition=%wide.region_6.7_spmd, body=%wide.region_5.6_spmd.sunk | while | flops 16390 | bytes 196751 | solution.py:30
  244.4 0.9 bitcast_add_fusion.6
  292.1 1.2 reduce-window_subtract_fusion
  293.9 1.2 fusion.10
  296.0 1.2 fusion.11
  297.2 1.0 pad_maximum_fusion
  298.2 2.4 copy.50
  300.6 5.9 %multiply_bitcast_fusion = f32[2048,384]{0,1:T(8,128)} fusion(bf16[1024,2048]{1,0:T(8,128)(2,1)} %param.7, bf16[48,8,8,128]{3,2,1,0:T(8,128)(2,1)} %bitcast.116), kind=kOutput, calls=%fused_computation.2 | convolution fusion | flops 1611399168 | bytes 8126464 | tf_op jit(solution)/shard_map/dot_general | solution.py:82
  306.5 3.6 copy.65
  311.1 1.4 fusion.4
  312.5 142.3 %reduce-scatter.4.cloned.1.call-done = f32[32,384]{1,0:T(8,128)} async-done(((f32[2048,384]{1,0:T(8,128)}), f32[32,384]{1,0:T(8,128)}) %reduce-scatter.4.cloned.1.call-update) | async-done | bytes 49168
  (90 shorter events, 55.8 us)
Async XLA Ops:
  7.2 62.7 %copy-start = (f32[1024,128]{1,0:T(8,128)S(1)}, f32[1024,128]{1,0:T(8,128)}, u32[]{:S(2)}) copy-start(f32[1024,128]{1,0:T(8,128)} %param.9) | copy-start | bytes 1572868
  7.2 144.0 %all-gather.5.cloned.1.call-start = ((), (), s32[]{:S(2)}) async-start(), calls=%async_computation.2 | async-start | bytes 4259840 | tf_op jit(solution)/shard_map/all_gather | solution.py:23
  69.8 166.7 %all-gather.7.cloned.1.call-start = ((), (), s32[]{:S(2)}) async-start(), calls=%async_computation.3 | async-start | bytes 4259840 | tf_op jit(solution)/shard_map/all_gather | solution.py:23
  72.3 382.4 %reduce-scatter.4.cloned.1.call-start = ((), (), s32[]{:S(2)}) async-start(), calls=%async_computation.4 | async-start | bytes 3194880
  79.9 212.2 %copy-start.6 = (f32[128,128]{1,0:T(8,128)S(1)}, f32[128,128]{1,0:T(8,128)}, u32[]{:S(2)}) copy-start(f32[128,128]{1,0:T(8,128)} %get-tuple-element.119) | copy-start | bytes 196612
  292.1 1.2 copy-start.5
  292.1 1.8 copy-start.4
  293.9 2.1 copy-start.3
  295.2 0.8 copy-start.1
  310.0 1.0 copy-start.2
Sparse Core Ops, SparseCore 0:
  69.9 81.2 all-gather.4
  154.5 81.9 all-gather.6
  310.2 144.5 reduce-scatter.3
